TPU v7x, 128 devices: a whole 4x4x4 slice. The times are simulated.
128 devices in a mesh: row: 16 (over z, x), col: 8 (over y, core).
Axes of the slice: x: 4, y: 4, z: 4, core: 2. Of those that a mesh axis runs over, the one named last changes fastest.
Arguments:
- coords: float32 [2048, 3, 512], P(('row', 'col')), may hold values from -1 to 258, as said below
- rhs: bfloat16 [2048, 16, 512], P(('row', 'col')), may hold values from -6 to 6
- near_pairs: int32 [8192, 2], P(('row', 'col')), may hold values from -1 to 128, as said below
- far_list: int32 [2048, 32], P(('row', 'col')), may hold values from 0 to 2047
- basis: bfloat16 [2048, 32, 512], P(('row', 'col')), may hold values from -0.25 to 0.25
- coupling: bfloat16 [2048, 32, 32, 32], P(('row', 'col')), may hold values from -1 to 1
Outputs:
- potential: float32 [2048, 16, 512], P(('row', 'col'))
Inputs may be any that keep to these rules, and one draw needn't show every extreme that they name: `near_pairs`: column 0 of a live slot names a local cluster (0 to 15); column 1 is -1 for an empty slot or o * 16 + l with the neighbour offset o (0 to 8) pointing inside the device grid. The second cluster of a live pair is the first one or one of the eight clusters next to it in the grid of clusters (device row times 16 plus local index, device column). Live slots of a device come first; one device has all 64 slots live; empty slots hold 0 in column 0. `coords`: cluster g with grid cell (i, j) = ((g // 16) // 8 * 16 + g % 16, (g // 16) % 8) has its panels in the box [i - 0.5, i + 1.5] x [j - 0.5, j + 1.5] x [0, 0.2].
All inputs are finite; a program needn't handle non-finite values.
Results may differ from a plain program's by a relative error of at most 0.003.
Values may be sent and summed in bfloat16 or wider, within the bound.
A program may use at most 64 MiB of HBM per device.

v0:
```python
import math

import jax
import jax.numpy as jnp
from jax import lax
from jax.sharding import PartitionSpec as P

COUPLE = 0.0625
SOFTEN = 0.0025


def padded(cells, sides, width):
    for axis, dim in sides:
        count = lax.axis_size(axis)
        ends = count - 1
        head = lax.slice_in_dim(cells, 0, width, axis=dim)
        tail = lax.slice_in_dim(cells, cells.shape[dim] - width, cells.shape[dim], axis=dim)
        cells = jnp.concatenate(
            [
                lax.ppermute(tail, axis, [(i, (i + 1) % count) for i in range(ends)]),
                cells,
                lax.ppermute(head, axis, [((i + 1) % count, i) for i in range(ends)]),
            ],
            axis=dim,
        )
    return cells


def from_behind(block, axis, distance):
    devices = range(lax.axis_size(axis))
    route = [(i - distance, i) for i in devices if i - distance in devices]
    return lax.ppermute(block, axis, route)


def tile_batch(first, second):
    delta_x = first[:, 0, :, None] - second[:, 0, None, :]
    delta_y = first[:, 1, :, None] - second[:, 1, None, :]
    delta_z = first[:, 2, :, None] - second[:, 2, None, :]
    squared = delta_x * delta_x + delta_y * delta_y + delta_z * delta_z
    return (COUPLE / jnp.sqrt(squared + SOFTEN)).astype(jnp.bfloat16)


def spread_terms(acc, targets, weights, terms):
    return acc.at[targets].add(terms * weights[:, None, None])


def per_device(coords, rhs, near_pairs, far_list, basis, coupling):
    width = coords.shape[0]
    sides = rhs.shape[1]
    panels = rhs.shape[2]
    rank = basis.shape[1]
    slots = near_pairs.shape[0]
    centre = 4 * width
    block = math.gcd(slots, 32)
    sources = padded(rhs[None, None], (("row", 0), ("col", 1)), 1)
    sources = sources.reshape(9 * width, sides, panels)
    points = padded(coords[None, None], (("row", 0), ("col", 1)), 1)
    points = points.reshape(9 * width, 3, panels)

    def pair_block(block_index, acc):
        entries = lax.dynamic_slice_in_dim(near_pairs, block_index * block, block, 0)
        left = entries[:, 0] + centre
        right_raw = entries[:, 1]
        alive = right_raw >= 0
        right = jnp.maximum(right_raw, 0)
        tiles = tile_batch(points[left], points[right])
        forward = jnp.einsum(
            "brq,bpq->brp", sources[right], tiles, preferred_element_type=jnp.float32
        )
        backward = jnp.einsum(
            "brp,bpq->brq", sources[left], tiles, preferred_element_type=jnp.float32
        )
        acc = spread_terms(acc, left, alive.astype(jnp.float32), forward)
        mirror = alive & (right != left)
        return spread_terms(acc, right, mirror.astype(jnp.float32), backward)

    sweep_end = slots // block
    start_acc = jnp.zeros((9 * width, sides, panels), jnp.float32)
    acc = lax.fori_loop(0, sweep_end, pair_block, start_acc)
    grid = acc.reshape(3, 3, width, sides, panels)
    by_rows = grid[:, 1]
    for step in (-1, 1):
        by_rows = by_rows + from_behind(grid[:, step + 1], "col", step)
    near = by_rows[1]
    for step in (-1, 1):
        near = near + from_behind(by_rows[step + 1], "row", step)
    coeffs = jnp.einsum("crp,ckp->crk", rhs, basis, preferred_element_type=jnp.float32).astype(
        jnp.bfloat16
    )
    flat_coeffs = coeffs.reshape(width, sides * rank)
    every = lax.all_gather(flat_coeffs, ("row", "col"), axis=0, tiled=True)
    picked = every[far_list].reshape(width, far_list.shape[1], sides, rank)
    inner = jnp.einsum("cfrk,cfkl->crl", picked, coupling, preferred_element_type=jnp.float32)
    far = jnp.einsum(
        "crl,clp->crp", inner.astype(jnp.bfloat16), basis, preferred_element_type=jnp.float32
    )
    return near + far


def solution(mesh):
    return jax.shard_map(
        per_device,
        mesh=mesh,
        in_specs=(
            P(("row", "col"), None, None),
            P(("row", "col"), None, None),
            P(("row", "col"), None),
            P(("row", "col"), None),
            P(("row", "col"), None, None),
            P(("row", "col"), None, None, None),
        ),
        out_specs=P(("row", "col"), None, None),
        check_vma=False,
    )
```

profile of v0, /device:TPU:104, one launch (start us, length us, event | category | flops | bytes accessed | tf_op | source)
XLA Modules:
  0.0 240.3 jit_solution(6370833392738759436)
XLA Ops:
  6.5 3.5 %collective-permute-start = (bf16[1,1,16,16,512]{4,3,2,1,0:T(8,128)(2,1)}, bf16[1,1,16,16,512]{4,3,2,1,0:T(8,128)(2,1)S(1)}, u32[]{:S(2)}, u32[]{:S(2)}) collective-permute-start(bf16[1,1,16,16,512]{4,3,2,1,0:T(8,128)(2,1)} %bitcast.96), channel_id=1, source_target_pairs={{0,8},{8,16},{16,24},{24,32},{32,40},{40,48},{48,56},{56,64},{64,7... | collective-permute-start | bytes 786440 | tf_op jit(solution)/shard_map/ppermute | solution.py:20
  10.1 4.6 %collective-permute-start.1 = (bf16[1,1,16,16,512]{4,3,2,1,0:T(8,128)(2,1)}, bf16[1,1,16,16,512]{4,3,2,1,0:T(8,128)(2,1)S(1)}, u32[]{:S(2)}, u32[]{:S(2)}) collective-permute-start(bf16[1,1,16,16,512]{4,3,2,1,0:T(8,128)(2,1)} %bitcast.97), channel_id=1, source_target_pairs={{8,0},{16,8},{24,16},{32,24},{40,32},{48,40},{56,48},{64,56},{72,6... | collective-permute-start | bytes 786440 | tf_op jit(solution)/shard_map/ppermute | solution.py:22
  14.6 4.3 %collective-permute-done = bf16[1,1,16,16,512]{4,3,2,1,0:T(8,128)(2,1)S(1)} collective-permute-done((bf16[1,1,16,16,512]{4,3,2,1,0:T(8,128)(2,1)}, bf16[1,1,16,16,512]{4,3,2,1,0:T(8,128)(2,1)S(1)}, u32[]{:S(2)}, u32[]{:S(2)}) %collective-permute-start) | collective-permute-done | bytes 262176 | tf_op jit(solution)/shard_map/ppermute | solution.py:20
  18.9 1.3 collective-permute-done.1
  20.2 1.9 pad_maximum_fusion.2
  22.1 1.9 collective-permute-start.2
  24.0 3.6 %collective-permute-start.3 = (bf16[3,1,16,16,512]{4,3,2,1,0:T(8,128)(2,1)}, bf16[3,1,16,16,512]{4,3,2,1,0:T(8,128)(2,1)}, u32[]{:S(2)}, u32[]{:S(2)}) collective-permute-start(bf16[3,1,16,16,512]{4,3,2,1,0:T(8,128)(2,1)} %pad_maximum_fusion.2), channel_id=1, source_target_pairs={{1,0},{2,1},{3,2},{4,3},{5,4},{6,5},{7,6},{9,8},{10,9},{11,10},{12... | collective-permute-start | bytes 2359304 | tf_op jit(solution)/shard_map/ppermute | solution.py:22
  27.7 3.1 %collective-permute-start.4 = (f32[1,1,16,3,512]{4,2,3,1,0:T(8,128)}, f32[1,1,16,3,512]{4,2,3,1,0:T(8,128)S(1)}, u32[]{:S(2)}, u32[]{:S(2)}) collective-permute-start(f32[1,1,16,3,512]{4,2,3,1,0:T(8,128)} %bitcast.112), channel_id=1, source_target_pairs={{0,8},{8,16},{16,24},{24,32},{32,40},{40,48},{48,56},{56,64},{64,7... | collective-permute-start | bytes 294920 | tf_op jit(solution)/shard_map/ppermute | solution.py:20
  30.8 5.2 %collective-permute-start.5 = (f32[1,1,16,3,512]{4,2,3,1,0:T(8,128)}, f32[1,1,16,3,512]{4,2,3,1,0:T(8,128)S(1)}, u32[]{:S(2)}, u32[]{:S(2)}) collective-permute-start(f32[1,1,16,3,512]{4,2,3,1,0:T(8,128)} %bitcast.113), channel_id=1, source_target_pairs={{8,0},{16,8},{24,16},{32,24},{40,32},{48,40},{56,48},{64,56},{72,6... | collective-permute-start | bytes 294920 | tf_op jit(solution)/shard_map/ppermute | solution.py:22
  36.0 1.2 collective-permute-done.4
  37.2 1.3 collective-permute-done.5
  38.5 0.9 pad_maximum_fusion.3
  39.4 1.9 collective-permute-start.6
  41.4 3.6 %collective-permute-start.7 = (f32[3,1,16,3,512]{4,2,3,1,0:T(8,128)S(1)}, f32[3,1,16,3,512]{4,2,3,1,0:T(8,128)S(1)}, u32[]{:S(2)}, u32[]{:S(2)}) collective-permute-start(f32[3,1,16,3,512]{4,2,3,1,0:T(8,128)S(1)} %pad_maximum_fusion.3), channel_id=1, source_target_pairs={{1,0},{2,1},{3,2},{4,3},{5,4},{6,5},{7,6},{9,8},{10,9},{11,10},{12... | collective-permute-start | bytes 884744 | tf_op jit(solution)/shard_map/ppermute | solution.py:22
  45.0 1.2 convolution_convert_fusion
  46.2 0.7 reshape.71
  47.0 0.5 collective-permute-done.6
  47.5 1.8 collective-permute-done.7
  49.2 1.0 pad_maximum_fusion.1
  50.2 0.6 copy.8
  50.9 2.6 %pad_maximum_fusion = bf16[3,3,16,16,512]{4,3,2,1,0:T(8,128)(2,1)} fusion(bf16[3,1,16,16,512]{4,3,2,1,0:T(8,128)(2,1)} %collective-permute-done.3, bf16[1,1,16,16,512]{4,3,2,1,0:T(8,128)(2,1)S(1)} %collective-permute-done.1, bf16[1,1,16,16,512]{4,3,2,1,0:T(8,128)(2,1)S(1)} %bitcast.99, bf16[1,1,16,16,512]{4,3,2,1,0:T(8,128)(2,1)S(1)} %collective-permute-done, ...), kind=kLoop, calls=%fused_computation.32 | loop fusion | flops 4718592 | bytes 4718592 | tf_op jit(solution)/shard_map/concatenate | solution.py:18
  53.4 2.8 %broadcast_in_dim.28 = f32[144,16,512]{2,1,0:T(8,128)} broadcast(f32[]{:T(128)} %constant.77.clone.1), dimensions={} | broadcast | bytes 4718596 | tf_op jit(solution)/shard_map/broadcast_in_dim | solution.py:78
  56.3 116.8 %while.15 = (s32[]{:T(128)}, f32[144,16,512]{2,1,0:T(8,128)}, s32[64,2]{0,1:T(2,128)S(1)}, bf16[144,16,512]{2,1,0:T(8,128)(2,1)}, f32[144,3,512]{2,1,0:T(4,128)S...) while((s32[]{:T(128)}, f32[144,16,512]{2,1,0:T(8,128)}, s32[64,2]{0,1:T(2,128)S(1)}, ...), condition=%wide.region_3.0_spmd, body=%wide.region_0.0_spmd.sunk | while | flops 722471296 | bytes 14691215 | solution.py:79
  56.3 0.7 gather_fusion.1
  57.1 0.1 fusion.36
  57.2 0.7 gather_fusion.2
  57.9 0.1 fusion.37
  58.1 0.6 copy.44
  58.8 0.6 copy.45
  59.4 2.3 gather_fusion
  61.6 0.5 fusion.38
  62.2 20.2 %fusion.39 = f32[32,16,512]{2,1,0:T(8,128)S(1)} fusion(bf16[32,16,512]{2,1,0:T(8,128)(2,1)S(1)} %gather_fusion, f32[32,512]{1,0:T(8,128)S(1)} %bitcast.100, f32[32,512]{1,0:T(8,128)S(1)} %bitcast.102, f32[32,512]{1,0:T(8,128)S(1)} %bitcast.104, f32[32,512]{1,0:T(8,128)S(1)} %bitcast.106, f32[32,512]{1,0:T(8,128)} %bitcast.108, ...), kind=kOutput, calls=%fused_computation.10.clone.1 | convolution fusion | flops 360972288 | bytes 1966208 | tf_op jit(solution)/shard_map/while/body/eval_jaxpr/brq,bpq->brp/dot_general | solution.py:67
  82.4 4.9 %scatter_fusion = f32[144,16,512]{2,1,0:T(8,128)} fusion(f32[144,16,512]{2,1,0:T(8,128)} %get-tuple-element.229, s32[32]{0:T(128)S(1)} %get-tuple-element.207, f32[32,16,512]{2,1,0:T(8,128)S(1)} %fusion.39), kind=kCustom, calls=%fused_computation.5.clone.1 | custom fusion | flops 262144 | bytes 3145856 | tf_op jit(solution)/shard_map/while/body/eval_jaxpr/scatter-add | solution.py:44
  87.3 2.3 gather_fusion.3
  89.6 19.6 %fusion.40 = f32[32,16,512]{2,1,0:T(8,128)S(1)} fusion(bf16[32,16,512]{2,1,0:T(8,128)(2,1)S(1)} %gather_fusion.3, f32[32,512]{1,0:T(8,128)S(1)} %bitcast.101, f32[32,512]{1,0:T(8,128)S(1)} %bitcast.103, f32[32,512]{1,0:T(8,128)S(1)} %bitcast.105, f32[32,512]{1,0:T(8,128)S(1)} %bitcast.107, f32[32,512]{1,0:T(8,128)} %bitcast.109, ...), kind=kOutput, calls=%fused_computation.11.clone.1 | convolution fusion | flops 360972288 | bytes 1966208 | tf_op jit(solution)/shard_map/while/body/eval_jaxpr/brp,bpq->brq/dot_general | solution.py:70
  109.3 5.0 %scatter_fusion.1 = f32[144,16,512]{2,1,0:T(8,128)} fusion(f32[144,16,512]{2,1,0:T(8,128)} %scatter_fusion, s32[32]{0:T(128)S(1)} %get-tuple-element.208, f32[32,16,512]{2,1,0:T(8,128)S(1)} %fusion.40), kind=kCustom, calls=%fused_computation.6.clone.1 | custom fusion | flops 262144 | bytes 3145856 | tf_op jit(solution)/shard_map/while/body/eval_jaxpr/scatter-add | solution.py:44
  114.3 0.7 gather_fusion.1
  115.2 0.7 gather_fusion.2
  115.9 0.1 fusion.37
  116.1 0.6 copy.44
  116.7 0.6 copy.45
  117.3 2.2 gather_fusion
  119.6 0.5 fusion.38
  120.1 20.2 %fusion.39 = f32[32,16,512]{2,1,0:T(8,128)S(1)} fusion(bf16[32,16,512]{2,1,0:T(8,128)(2,1)S(1)} %gather_fusion, f32[32,512]{1,0:T(8,128)S(1)} %bitcast.100, f32[32,512]{1,0:T(8,128)S(1)} %bitcast.102, f32[32,512]{1,0:T(8,128)S(1)} %bitcast.104, f32[32,512]{1,0:T(8,128)S(1)} %bitcast.106, f32[32,512]{1,0:T(8,128)} %bitcast.108, ...), kind=kOutput, calls=%fused_computation.10.clone.1 | convolution fusion | flops 360972288 | bytes 1966208 | tf_op jit(solution)/shard_map/while/body/eval_jaxpr/brq,bpq->brp/dot_general | solution.py:67
  140.4 5.4 %scatter_fusion = f32[144,16,512]{2,1,0:T(8,128)} fusion(f32[144,16,512]{2,1,0:T(8,128)} %get-tuple-element.229, s32[32]{0:T(128)S(1)} %get-tuple-element.207, f32[32,16,512]{2,1,0:T(8,128)S(1)} %fusion.39), kind=kCustom, calls=%fused_computation.5.clone.1 | custom fusion | flops 262144 | bytes 3145856 | tf_op jit(solution)/shard_map/while/body/eval_jaxpr/scatter-add | solution.py:44
  145.8 2.2 gather_fusion.3
  148.0 19.6 %fusion.40 = f32[32,16,512]{2,1,0:T(8,128)S(1)} fusion(bf16[32,16,512]{2,1,0:T(8,128)(2,1)S(1)} %gather_fusion.3, f32[32,512]{1,0:T(8,128)S(1)} %bitcast.101, f32[32,512]{1,0:T(8,128)S(1)} %bitcast.103, f32[32,512]{1,0:T(8,128)S(1)} %bitcast.105, f32[32,512]{1,0:T(8,128)S(1)} %bitcast.107, f32[32,512]{1,0:T(8,128)} %bitcast.109, ...), kind=kOutput, calls=%fused_computation.11.clone.1 | convolution fusion | flops 360972288 | bytes 1966208 | tf_op jit(solution)/shard_map/while/body/eval_jaxpr/brp,bpq->brq/dot_general | solution.py:70
  167.7 5.4 %scatter_fusion.1 = f32[144,16,512]{2,1,0:T(8,128)} fusion(f32[144,16,512]{2,1,0:T(8,128)} %scatter_fusion, s32[32]{0:T(128)S(1)} %get-tuple-element.208, f32[32,16,512]{2,1,0:T(8,128)S(1)} %fusion.40), kind=kCustom, calls=%fused_computation.6.clone.1 | custom fusion | flops 262144 | bytes 3145856 | tf_op jit(solution)/shard_map/while/body/eval_jaxpr/scatter-add | solution.py:44
  173.1 4.2 %slice_bitcast_fusion.1 = (f32[3,16,16,512]{3,2,1,0:T(8,128)}, f32[3,16,16,512]{3,2,1,0:T(8,128)}) fusion(f32[3,3,16,16,512]{4,3,2,1,0:T(8,128)} %bitcast.93), kind=kLoop, calls=%fused_computation.34 | loop fusion | bytes 6291456 | tf_op jit(solution)/shard_map/squeeze | solution.py:83
  177.2 3.7 %collective-permute-start.8 = (f32[3,16,16,512]{3,2,1,0:T(8,128)}, f32[3,16,16,512]{3,2,1,0:T(8,128)S(1)}, u32[]{:S(2)}, u32[]{:S(2)}) collective-permute-start(f32[3,16,16,512]{3,2,1,0:T(8,128)} %get-tuple-element.160), channel_id=1, source_target_pairs={{1,0},{2,1},{3,2},{4,3},{5,4},{6,5},{7,6},{9,8},{10,9},{11,10},{12... | collective-permute-start | bytes 4718600 | tf_op jit(solution)/shard_map/ppermute | solution.py:32
  180.9 1.9 collective-permute-start.9
  182.9 16.2 %collective-permute-done.8 = f32[3,16,16,512]{3,2,1,0:T(8,128)S(1)} collective-permute-done((f32[3,16,16,512]{3,2,1,0:T(8,128)}, f32[3,16,16,512]{3,2,1,0:T(8,128)S(1)}, u32[]{:S(2)}, u32[]{:S(2)}) %collective-permute-start.8) | collective-permute-done | bytes 1572896 | tf_op jit(solution)/shard_map/ppermute | solution.py:32
  199.1 3.8 %collective-permute-done.9 = f32[3,16,16,512]{3,2,1,0:T(8,128)} collective-permute-done((f32[3,16,16,512]{3,2,1,0:T(8,128)}, f32[3,16,16,512]{3,2,1,0:T(8,128)}, u32[]{:S(2)}, u32[]{:S(2)}) %collective-permute-start.9) | collective-permute-done | bytes 1572896 | tf_op jit(solution)/shard_map/ppermute | solution.py:32
  202.9 2.4 %fusion.12 = f32[3,16,16,512]{3,2,1,0:T(8,128)S(1)} fusion(f32[3,16,16,512]{3,2,1,0:T(8,128)} %collective-permute-done.9, f32[3,16,16,512]{3,2,1,0:T(8,128)S(1)} %collective-permute-done.8, f32[3,3,16,16,512]{4,3,2,1,0:T(8,128)} %bitcast.94), kind=kLoop, calls=%fused_computation.37 | loop fusion | flops 786432 | bytes 6291456 | tf_op jit(solution)/shard_map/add | solution.py:83
  205.4 1.1 copy-done.1
  206.5 1.0 slice_bitcast_fusion.4
  207.5 4.9 %collective-permute-start.10 = (f32[16,16,512]{2,1,0:T(8,128)}, f32[16,16,512]{2,1,0:T(8,128)}, u32[]{:S(2)}, u32[]{:S(2)}) collective-permute-start(f32[16,16,512]{2,1,0:T(8,128)} %get-tuple-element.162), channel_id=1, source_target_pairs={{8,0},{16,8},{24,16},{32,24},{40,32},{48,40},{56,48},{64,56},{72,6... | collective-permute-start | bytes 1572872 | tf_op jit(solution)/shard_map/ppermute | solution.py:32
  212.4 1.9 collective-permute-start.11
  214.4 3.8 %gather_fusion.4 = bf16[512,512]{1,0:T(8,128)(2,1)S(1)} fusion(bf16[2048,512]{1,0:T(8,128)(2,1)} %all-gather.2.cloned.1.call-done, s32[1024]{0:T(1024)S(1)} %pad_clamp_fusion.2), kind=kCustom, calls=%fused_computation.4 | custom fusion | bytes 1050624 | tf_op jit(solution)/shard_map/gather | solution.py:92
  218.2 1.2 reshape.72
  219.5 3.7 %fusion.14 = f32[16,16,512]{2,1,0:T(8,128)S(1)} fusion(bf16[16,32,512]{2,1,0:T(8,128)(2,1)S(1)} %copy-done, bf16[16,32,16,32]{3,2,1,0:T(8,128)(2,1)S(1)} %reshape.72, bf16[16,32,32,32]{3,2,1,0:T(8,128)(2,1)} %param.13), kind=kOutput, calls=%fused_computation.41 | convolution fusion | flops 25174016 | bytes 2621440 | tf_op jit(solution)/shard_map/crl,clp->crp/dot_general | solution.py:94
  223.2 1.7 collective-permute-done.10
  224.9 6.2 %collective-permute-done.11 = f32[16,16,512]{2,1,0:T(8,128)} collective-permute-done((f32[16,16,512]{2,1,0:T(8,128)}, f32[16,16,512]{2,1,0:T(8,128)}, u32[]{:S(2)}, u32[]{:S(2)}) %collective-permute-start.11) | collective-permute-done | bytes 524320 | tf_op jit(solution)/shard_map/ppermute | solution.py:32
  231.1 2.4 fusion.17
  (32 shorter events, 0.5 us)
Async XLA Ops:
  6.5 38.5 %copy-start = (bf16[16,32,512]{2,1,0:T(8,128)(2,1)S(1)}, bf16[16,32,512]{2,1,0:T(8,128)(2,1)}, u32[]{:S(2)}) copy-start(bf16[16,32,512]{2,1,0:T(8,128)(2,1)} %param.12) | copy-start | bytes 1572868
  6.5 44.3 %copy-start.2 = (bf16[16,16,512]{2,1,0:T(8,128)(2,1)S(1)}, bf16[16,16,512]{2,1,0:T(8,128)(2,1)}, u32[]{:S(2)}) copy-start(bf16[16,16,512]{2,1,0:T(8,128)(2,1)} %param.9) | copy-start | bytes 786436
  6.5 207.8 %all-gather.2.cloned.1.call-start = ((), (), s32[]{:S(2)}) async-start(), calls=%async_computation | async-start | bytes 2113536 | tf_op jit(solution)/shard_map/all_gather | solution.py:91
  6.5 12.4 %collective-permute-start = (bf16[1,1,16,16,512]{4,3,2,1,0:T(8,128)(2,1)}, bf16[1,1,16,16,512]{4,3,2,1,0:T(8,128)(2,1)S(1)}, u32[]{:S(2)}, u32[]{:S(2)}) collective-permute-start(bf16[1,1,16,16,512]{4,3,2,1,0:T(8,128)(2,1)} %bitcast.96), channel_id=1, source_target_pairs={{0,8},{8,16},{16,24},{24,32},{32,40},{40,48},{48,56},{56,64},{64,7... | collective-permute-start | bytes 786440 | tf_op jit(solution)/shard_map/ppermute | solution.py:20
  10.1 10.1 %collective-permute-start.1 = (bf16[1,1,16,16,512]{4,3,2,1,0:T(8,128)(2,1)}, bf16[1,1,16,16,512]{4,3,2,1,0:T(8,128)(2,1)S(1)}, u32[]{:S(2)}, u32[]{:S(2)}) collective-permute-start(bf16[1,1,16,16,512]{4,3,2,1,0:T(8,128)(2,1)} %bitcast.97), channel_id=1, source_target_pairs={{8,0},{16,8},{24,16},{32,24},{40,32},{48,40},{56,48},{64,56},{72,6... | collective-permute-start | bytes 786440 | tf_op jit(solution)/shard_map/ppermute | solution.py:22
  22.1 28.7 %collective-permute-start.2 = (bf16[3,1,16,16,512]{4,3,2,1,0:T(8,128)(2,1)}, bf16[3,1,16,16,512]{4,3,2,1,0:T(8,128)(2,1)S(1)}, u32[]{:S(2)}, u32[]{:S(2)}) collective-permute-start(bf16[3,1,16,16,512]{4,3,2,1,0:T(8,128)(2,1)} %pad_maximum_fusion.2), channel_id=1, source_target_pairs={{0,1},{1,2},{2,3},{3,4},{4,5},{5,6},{6,7},{8,9},{9,10},{10,11},{11... | collective-permute-start | bytes 2359304 | tf_op jit(solution)/shard_map/ppermute | solution.py:20
  24.0 26.8 %collective-permute-start.3 = (bf16[3,1,16,16,512]{4,3,2,1,0:T(8,128)(2,1)}, bf16[3,1,16,16,512]{4,3,2,1,0:T(8,128)(2,1)}, u32[]{:S(2)}, u32[]{:S(2)}) collective-permute-start(bf16[3,1,16,16,512]{4,3,2,1,0:T(8,128)(2,1)} %pad_maximum_fusion.2), channel_id=1, source_target_pairs={{1,0},{2,1},{3,2},{4,3},{5,4},{6,5},{7,6},{9,8},{10,9},{11,10},{12... | collective-permute-start | bytes 2359304 | tf_op jit(solution)/shard_map/ppermute | solution.py:22
  27.7 9.5 %collective-permute-start.4 = (f32[1,1,16,3,512]{4,2,3,1,0:T(8,128)}, f32[1,1,16,3,512]{4,2,3,1,0:T(8,128)S(1)}, u32[]{:S(2)}, u32[]{:S(2)}) collective-permute-start(f32[1,1,16,3,512]{4,2,3,1,0:T(8,128)} %bitcast.112), channel_id=1, source_target_pairs={{0,8},{8,16},{16,24},{24,32},{32,40},{40,48},{48,56},{56,64},{64,7... | collective-permute-start | bytes 294920 | tf_op jit(solution)/shard_map/ppermute | solution.py:20
  30.8 7.7 %collective-permute-start.5 = (f32[1,1,16,3,512]{4,2,3,1,0:T(8,128)}, f32[1,1,16,3,512]{4,2,3,1,0:T(8,128)S(1)}, u32[]{:S(2)}, u32[]{:S(2)}) collective-permute-start(f32[1,1,16,3,512]{4,2,3,1,0:T(8,128)} %bitcast.113), channel_id=1, source_target_pairs={{8,0},{16,8},{24,16},{32,24},{40,32},{48,40},{56,48},{64,56},{72,6... | collective-permute-start | bytes 294920 | tf_op jit(solution)/shard_map/ppermute | solution.py:22
  39.4 8.0 %collective-permute-start.6 = (f32[3,1,16,3,512]{4,2,3,1,0:T(8,128)S(1)}, f32[3,1,16,3,512]{4,2,3,1,0:T(8,128)S(1)}, u32[]{:S(2)}, u32[]{:S(2)}) collective-permute-start(f32[3,1,16,3,512]{4,2,3,1,0:T(8,128)S(1)} %pad_maximum_fusion.3), channel_id=1, source_target_pairs={{0,1},{1,2},{2,3},{3,4},{4,5},{5,6},{6,7},{8,9},{9,10},{10,11},{11... | collective-permute-start | bytes 884744 | tf_op jit(solution)/shard_map/ppermute | solution.py:20
  41.4 7.9 %collective-permute-start.7 = (f32[3,1,16,3,512]{4,2,3,1,0:T(8,128)S(1)}, f32[3,1,16,3,512]{4,2,3,1,0:T(8,128)S(1)}, u32[]{:S(2)}, u32[]{:S(2)}) collective-permute-start(f32[3,1,16,3,512]{4,2,3,1,0:T(8,128)S(1)} %pad_maximum_fusion.3), channel_id=1, source_target_pairs={{1,0},{2,1},{3,2},{4,3},{5,4},{6,5},{7,6},{9,8},{10,9},{11,10},{12... | collective-permute-start | bytes 884744 | tf_op jit(solution)/shard_map/ppermute | solution.py:22
  50.8 5.4 %copy-start.3 = (s32[64,2]{0,1:T(2,128)S(1)}, s32[64,2]{0,1:T(2,128)}, u32[]{:S(2)}) copy-start(s32[64,2]{0,1:T(2,128)} %param.10) | copy-start | bytes 1540
  173.1 9.8 %copy-start.4 = (s32[16,32]{1,0:T(8,128)S(1)}, s32[16,32]{1,0:T(8,128)}, u32[]{:S(2)}) copy-start(s32[16,32]{1,0:T(8,128)} %param.11) | copy-start | bytes 6148
  177.2 21.9 %collective-permute-start.8 = (f32[3,16,16,512]{3,2,1,0:T(8,128)}, f32[3,16,16,512]{3,2,1,0:T(8,128)S(1)}, u32[]{:S(2)}, u32[]{:S(2)}) collective-permute-start(f32[3,16,16,512]{3,2,1,0:T(8,128)} %get-tuple-element.160), channel_id=1, source_target_pairs={{1,0},{2,1},{3,2},{4,3},{5,4},{6,5},{7,6},{9,8},{10,9},{11,10},{12... | collective-permute-start | bytes 4718600 | tf_op jit(solution)/shard_map/ppermute | solution.py:32
  180.9 22.1 %collective-permute-start.9 = (f32[3,16,16,512]{3,2,1,0:T(8,128)}, f32[3,16,16,512]{3,2,1,0:T(8,128)}, u32[]{:S(2)}, u32[]{:S(2)}) collective-permute-start(f32[3,16,16,512]{3,2,1,0:T(8,128)} %get-tuple-element.161), channel_id=1, source_target_pairs={{0,1},{1,2},{2,3},{3,4},{4,5},{5,6},{6,7},{8,9},{9,10},{10,11},{11... | collective-permute-start | bytes 4718600 | tf_op jit(solution)/shard_map/ppermute | solution.py:32
  205.4 1.1 copy-start.1
  207.5 17.3 %collective-permute-start.10 = (f32[16,16,512]{2,1,0:T(8,128)}, f32[16,16,512]{2,1,0:T(8,128)}, u32[]{:S(2)}, u32[]{:S(2)}) collective-permute-start(f32[16,16,512]{2,1,0:T(8,128)} %get-tuple-element.162), channel_id=1, source_target_pairs={{8,0},{16,8},{24,16},{32,24},{40,32},{48,40},{56,48},{64,56},{72,6... | collective-permute-start | bytes 1572872 | tf_op jit(solution)/shard_map/ppermute | solution.py:32
  212.4 18.7 %collective-permute-start.11 = (f32[16,16,512]{2,1,0:T(8,128)}, f32[16,16,512]{2,1,0:T(8,128)}, u32[]{:S(2)}, u32[]{:S(2)}) collective-permute-start(f32[16,16,512]{2,1,0:T(8,128)} %get-tuple-element.163), channel_id=1, source_target_pairs={{0,8},{8,16},{16,24},{24,32},{32,40},{40,48},{48,56},{56,64},{64,7... | collective-permute-start | bytes 1572872 | tf_op jit(solution)/shard_map/ppermute | solution.py:32
Sparse Core Ops, SparseCore 0:
  47.1 65.8 all-gather.1
where the time goes:
time: 242 us; the launch traced here: 240 us
  matrix products  84.6 us (35%)
  starting transfers between devices  39.9 us (16%)
  waiting for transfers between devices  38.3 us (16%)
  other arithmetic  33 us (14%)
  local copies, waits for them, and re-layouts  30.7 us (13%)
  between operations  13.6 us (6%)
    dot_general x2, matrix products, pair_block(): jnp.einsum('brq,bpq->brp', sources[right], tiles, preferred_element_type=...  40.4 us
    dot_general x2, matrix products, pair_block(): jnp.einsum('brp,bpq->brq', sources[left], tiles, preferred_element_type=j...  39.2 us
    ppermute x4, waiting for transfers between devices, from_behind(): return lax.ppermute(block, axis, route)  27.9 us
    scatter-add x4, other arithmetic, spread_terms(): return acc.at[targets].add(terms * weights[:, None, None])  20.7 us
    ppermute x4, starting transfers between devices, padded(): lax.ppermute(head, axis, [((i + 1) % count, i) for i in range(ends)])  17 us
    ppermute x4, starting transfers between devices, from_behind(): return lax.ppermute(block, axis, route)  12.4 us
    ppermute x4, starting transfers between devices, padded(): lax.ppermute(tail, axis, [(i, (i + 1) % count) for i in range(ends)])  10.5 us
    concatenate x4, other arithmetic, padded(): jnp.concatenate([lax.ppermute(tail, axis, [(i, (i + 1) % count) for i in...  6.35 us
  transfers between devices with their start and end apart: 13, of which 10 were waited for; matrix products, arithmetic and copies ran while one was open for 59% of the time, Pallas kernels for 0%

commit v1 on v0

v1 whole, which is shorter than its diff:
```python
import functools

import jax
import jax.numpy as jnp
from jax import lax
from jax.experimental import pallas as pl
from jax.experimental.pallas import tpu as pltpu
from jax.sharding import PartitionSpec as P

MESH = pl.DeviceIdType.MESH
BF = jnp.bfloat16
F32 = jnp.float32
SOFTEN = 0.0025
GAIN = 256.0

NR, NC = 16, 8
CL, R, PS, K, FAR, NP = 16, 16, 512, 32, 32, 64
CHUNK = 64
NEIGHBOURS = [(0, -1), (0, 1), (-1, -1), (-1, 0), (-1, 1), (1, -1), (1, 0), (1, 1)]


def place(row, col):
    return (lax.rem(row + NR, NR), lax.rem(col + NC, NC))


def pair_ids(pairs, s):
    a = pairs[0, s]
    b = pairs[1, s]
    b = jnp.where(b < 0, 4 * CL + a, b)
    o = b // CL
    l = b % CL
    drow = o // 3 - 1
    wc = o % 3
    wr = jnp.clip(1 + drow * CL + l, 0, CL + 1)
    return a, wc, wr


def make_tile(s, tile, pairs, tables, wc_ref, row0, col0):
    a, wc, wr = pair_ids(pairs, s)
    x0 = (row0 * CL + a).astype(F32) + 0.5
    y0 = col0.astype(F32) + 0.5
    at = pl.ds(wr + 7, 1)
    bx = wc_ref[wc, 0, at, :] - x0
    by = wc_ref[wc, 1, at, :] - y0
    bz = wc_ref[wc, 2, at, :]
    nb = GAIN * (bx * bx + by * by + bz * bz + SOFTEN)
    bx, by, bz = (-2.0 * GAIN) * bx, (-2.0 * GAIN) * by, (-2.0 * GAIN) * bz
    bx, by, bz, nb = [jnp.broadcast_to(v, (8, PS)) for v in (bx, by, bz, nb)]
    for p in range(0, PS, 16):
        for q in range(0, PS, 128):
            ql = slice(q, q + 128)
            halves = []
            for h in (p, p + 8):
                ax, ay, az, na = [tables[a, i, h : h + 8, :] for i in range(4)]
                sq = (na + nb[:, ql]) + ax * bx[:, ql]
                sq = sq + (ay * by[:, ql] + az * bz[:, ql])
                halves.append(lax.rsqrt(sq))
            tile[p : p + 16, ql] = jnp.concatenate(halves, axis=0).astype(BF)


def use_tile(s, tile, pairs, wr_ref, f_ref, b_ref):
    a, wc, wr = pair_ids(pairs, s)
    left = wr_ref[1, a + 1]
    right = wr_ref[wc, wr]
    t = tile[...]
    rows = pl.ds(pl.multiple_of(s * R, R), R)
    f_ref[rows, :] = lax.dot_general(
        right, t, (((1,), (1,)), ((), ())), preferred_element_type=F32
    ).astype(BF)
    b_ref[rows, :] = jnp.dot(left, t, preferred_element_type=F32).astype(BF)


def one_hot(codes, first, count):
    rows = lax.broadcasted_iota(jnp.int32, (count, NP * R), 0) + first
    return jnp.where(rows == codes, 1.0, 0.0).astype(BF)


def slot_codes(pairs_v):
    a = pairs_v[0:1, :]
    b = pairs_v[1:2, :]
    alive = b >= 0
    b = jnp.maximum(b, 0)
    o = lax.shift_right_logical(b, 4)
    l = lax.bitwise_and(b, 15)
    down = jnp.where(o >= 6, 2, jnp.where(o >= 3, 1, 0))
    wc = o - 3 * down
    wr = (down - 1) * CL + l + 1
    same = jnp.logical_and(o == 4, l == a)
    fwd = jnp.where(alive, a, -1)
    bwd = jnp.where(jnp.logical_and(alive, jnp.logical_not(same)), wc * (CL + 2) + wr, -1)
    slot = lax.broadcasted_iota(jnp.int32, (NP, NP * R), 0)
    lane = lax.broadcasted_iota(jnp.int32, (NP, NP * R), 1)
    spread = jnp.where(lax.shift_right_logical(lane, 4) == slot, 1.0, 0.0).astype(BF)
    inner = lax.bitwise_and(lax.broadcasted_iota(jnp.int32, (1, NP * R), 1), 15)
    out = []
    for v in (fwd, bwd):
        v = jnp.broadcast_to(v, (8, NP)).astype(F32).astype(BF)
        v = jnp.dot(v, spread, preferred_element_type=F32)[0:1, :]
        out.append(v.astype(jnp.int32) * R + inner)
    return out


def body(
    pairs, far, pairs_v, coords, rhs, basis, coupling, out,
    own_c, wc_ref, wr_ref, bas, cpl, tables, every, tile0, tile1, f_ref, b_ref,
    send, back_c, back_r,
    loc_sem, hs_sem, hr_sem, g1s, g1r, g2s, g2r, g3s, g3r, bs_sem, br_sem,
):
    row = lax.axis_index("row")
    col = lax.axis_index("col")
    core = lax.rem(col, 2)
    cy = col // 2

    loads = [
        pltpu.make_async_copy(coords, own_c, loc_sem.at[0]),
        pltpu.make_async_copy(rhs, wr_ref.at[1, pl.ds(1, CL)], loc_sem.at[1]),
        pltpu.make_async_copy(basis, bas, loc_sem.at[2]),
        pltpu.make_async_copy(coupling, cpl, loc_sem.at[3]),
        pltpu.make_async_copy(coords, wc_ref.at[1, :, pl.ds(8, CL)], loc_sem.at[4]),
    ]
    for c in loads:
        c.start()

    barrier = pltpu.get_barrier_semaphore()
    partners = [place(row + dr, col + dc) for dr, dc in NEIGHBOURS if dc]
    partners += [place(row, col + 2 * k) for k in (1, 2, 3)]
    partners += [place(row + k, col) for k in range(1, NR)]
    for target in partners:
        pl.semaphore_signal(barrier, inc=1, device_id=target, device_id_type=MESH)
    pl.semaphore_wait(barrier, len(partners))

    def remote(src, dst, s, r, target):
        return pltpu.make_async_remote_copy(
            src_ref=src, dst_ref=dst, send_sem=s, recv_sem=r, device_id=target, device_id_type=MESH
        )

    halo = []
    for k, (dr, dc) in enumerate(NEIGHBOURS):
        target = place(row + dr, col + dc)
        if dr == 0:
            pieces = [
                (rhs, wr_ref.at[1 - dc, pl.ds(1, CL)]),
                (coords, wc_ref.at[1 - dc, :, pl.ds(8, CL)]),
            ]
        elif dr == 1:
            pieces = [
                (rhs.at[pl.ds(CL - 1, 1)], wr_ref.at[1 - dc, pl.ds(0, 1)]),
                (coords.at[:, pl.ds(CL - 8, 8)], wc_ref.at[1 - dc, :, pl.ds(0, 8)]),
            ]
        else:
            pieces = [
                (rhs.at[pl.ds(0, 1)], wr_ref.at[1 - dc, pl.ds(CL + 1, 1)]),
                (coords.at[:, pl.ds(0, 8)], wc_ref.at[1 - dc, :, pl.ds(CL + 8, 8)]),
            ]
        for i, (src, dst) in enumerate(pieces):
            halo.append(remote(src, dst, hs_sem.at[k, i], hr_sem.at[k, i], target))
    for c in halo:
        c.start()

    loads[1].wait()
    loads[2].wait()
    lane_of = lax.shift_right_logical(lax.broadcasted_iota(jnp.int32, (R, 4 * K), 1), 5)
    for j in range(CL // 4):
        left = wr_ref[1, 1 + 4 * j : 5 + 4 * j].reshape(4 * R, PS)
        right = bas[4 * j : 4 * j + 4].reshape(4 * K, PS)
        full = lax.dot_general(left, right, (((1,), (1,)), ((), ())), preferred_element_type=F32)
        mine = jnp.zeros((R, 4 * K), F32)
        for i in range(4):
            mine = mine + jnp.where(lane_of == i, full[i * R : (i + 1) * R, :], 0.0)
        every[row, cy, core, j] = mine.astype(BF)

    first = []
    for k in (1, 2, 3):
        ref = every.at[row, cy, core]
        first.append(remote(ref, ref, g1s.at[k - 1], g1r.at[k - 1], place(row, col + 2 * k)))
    for c in first:
        c.start()

    loads[0].wait()
    steps = lax.broadcasted_iota(jnp.int32, (CL, PS), 0) + row * CL
    ox = own_c[0] - (steps.astype(F32) + 0.5)
    oy = own_c[1] - (col.astype(F32) + 0.5)
    oz = own_c[2]
    on = GAIN * (ox * ox + oy * oy + oz * oz)
    for i, v in enumerate((ox, oy, oz, on)):
        v = v.T
        for g in range(CL):
            tables[g, i] = jnp.broadcast_to(v[:, g : g + 1], (PS, 128))

    for c in first:
        c.wait()
    second = []
    for k in range(1, NR):
        ref = every.at[row, :, core]
        second.append(remote(ref, ref, g2s.at[k - 1], g2r.at[k - 1], place(row + k, col)))
    for c in second:
        c.start()

    loads[4].wait()
    for c in halo:
        c.wait()

    tiles = (tile0, tile1)
    build = functools.partial(
        make_tile, pairs=pairs, tables=tables, wc_ref=wc_ref, row0=row, col0=col
    )
    use = functools.partial(use_tile, pairs=pairs, wr_ref=wr_ref, f_ref=f_ref, b_ref=b_ref)

    def sweep(lo, hi):
        @pl.loop(lo, hi)
        def _(i):
            for j in range(2):

                @pl.when(i < NP + j)
                def _():
                    s = 2 * i + j
                    use(s, tiles[j])
                    build(jnp.minimum(s + 1, NP - 1), tiles[1 - j])

    build(0, tile0)
    cut = NP // 2 * 3 // 4
    sweep(0, cut)
    for c in second:
        c.wait()
    ref = every.at[:, :, core]
    third = remote(ref, ref, g3s.at[0], g3r.at[0], (row, col + 1 - 2 * core))
    third.start()
    sweep(cut, NP // 2)

    fwd, bwd = slot_codes(pairs_v)
    terms = b_ref[...]
    back = []

    def give(k):
        dr, dc = NEIGHBOURS[k]
        target = place(row + dr, col + dc)
        if dr == 0:
            src, dst = send.at[dc + 1, pl.ds(1, CL)], back_c.at[k]
        else:
            src = send.at[dc + 1, pl.ds(0 if dr < 0 else CL + 1, 1)]
            dst = back_r.at[pl.ds(k - 2, 1)]
        c = remote(src, dst, bs_sem.at[k], br_sem.at[k], target)
        c.start()
        back.append(c)

    wide = (CL + 2) * R
    for dc, ks in ((-1, (0, 2, 5)), (1, (1, 4, 7))):
        part = jnp.dot(one_hot(bwd, (dc + 1) * wide, wide), terms, preferred_element_type=F32)
        send[dc + 1] = part.astype(BF).reshape(CL + 2, R, PS)
        for k in ks:
            give(k)
    for at, k in ((0, 3), (CL + 1, 6)):
        part = jnp.dot(one_hot(bwd, wide + at * R, R), terms, preferred_element_type=F32)
        send[1, at] = part.astype(BF)
        give(k)
    near = jnp.dot(one_hot(bwd, wide + R, CL * R), terms, preferred_element_type=F32)
    near = near + jnp.dot(one_hot(fwd, 0, CL * R), f_ref[...], preferred_element_type=F32)
    out[...] = near.reshape(CL, R, PS)

    third.wait()
    loads[3].wait()

    @pl.loop(0, CL)
    def _(g):
        blocks = []
        for f in range(0, FAR, 4):
            mine = jnp.zeros((R, 4 * K), F32)
            for j in range(4):
                h = far[g, f + j]
                d = h // CL
                got = every[d // NC, (d % NC) // 2, d % 2, (h % CL) // 4].astype(F32)
                got = pltpu.roll(got, ((j - h % 4 + 4) % 4) * K, 1)
                mine = jnp.where(lane_of == j, got, mine)
            blocks.append(mine.astype(BF))
        z = jnp.dot(jnp.concatenate(blocks, axis=1), cpl[g], preferred_element_type=F32)
        out[g] += jnp.dot(z.astype(BF), bas[g], preferred_element_type=F32)

    for c in back:
        c.wait()
    out[...] += back_c[0].astype(F32) + back_c[1].astype(F32)
    out[CL - 1] += back_r[0].astype(F32) + back_r[1].astype(F32) + back_r[2].astype(F32)
    out[0] += back_r[3].astype(F32) + back_r[4].astype(F32) + back_r[5].astype(F32)


def per_device(coords, rhs, near_pairs, far_list, basis, coupling):
    smem = pl.BlockSpec(memory_space=pltpu.SMEM)
    vmem = pl.BlockSpec(memory_space=pltpu.VMEM)
    hbm = pl.BlockSpec(memory_space=pl.ANY)
    dma = pltpu.SemaphoreType.DMA
    pairs = near_pairs.T
    return pl.pallas_call(
        body,
        out_shape=jax.ShapeDtypeStruct((CL, R, PS), F32),
        in_specs=[smem, smem, vmem, hbm, hbm, hbm, hbm],
        out_specs=vmem,
        scratch_shapes=[
            pltpu.VMEM((3, CL, PS), F32),
            pltpu.VMEM((3, 3, CL + 16, PS), F32),
            pltpu.VMEM((3, CL + 2, R, PS), BF),
            pltpu.VMEM((CL, K, PS), BF),
            pltpu.VMEM((CL, FAR * K, K), BF),
            pltpu.VMEM((CL, 4, PS, 128), F32),
            pltpu.VMEM((NR, NC // 2, 2, CL // 4, R, 4 * K), BF),
            pltpu.VMEM((PS, PS), BF),
            pltpu.VMEM((PS, PS), BF),
            pltpu.VMEM((NP * R, PS), BF),
            pltpu.VMEM((NP * R, PS), BF),
            pltpu.VMEM((3, CL + 2, R, PS), BF),
            pltpu.VMEM((2, CL, R, PS), BF),
            pltpu.VMEM((6, R, PS), BF),
            dma((5,)),
            dma((8, 2)),
            dma((8, 2)),
            dma((3,)),
            dma((3,)),
            dma((NR - 1,)),
            dma((NR - 1,)),
            dma((1,)),
            dma((1,)),
            dma((8,)),
            dma((8,)),
        ],
        compiler_params=pltpu.CompilerParams(
            collective_id=0, has_side_effects=True, vmem_limit_bytes=52 * 2**20
        ),
        name="hmatrix",
    )(
        pairs,
        far_list,
        pairs,
        coords.transpose(1, 0, 2),
        rhs,
        basis,
        coupling.reshape(CL, FAR * K, K),
    )


def solution(mesh):
    return jax.shard_map(
        per_device,
        mesh=mesh,
        in_specs=(
            P(("row", "col"), None, None),
            P(("row", "col"), None, None),
            P(("row", "col"), None),
            P(("row", "col"), None),
            P(("row", "col"), None, None),
            P(("row", "col"), None, None, None),
        ),
        out_specs=P(("row", "col"), None, None),
        check_vma=False,
    )
```

time: 242 us -> 69.2 us (0.29)
  the two profiles are of different devices: /device:TPU:104 before, /device:TPU:1 now
where the time goes in v1:
time: 69.2 us; the launch traced here: 69 us
  Pallas kernels  63.9 us (92%)
  local copies, waits for them, and re-layouts  5.05 us (7%)
    pallas_call x1, Pallas kernels, per_device(): pl.pallas_call(body, out_shape=jax.ShapeDtypeStruct((CL, R, PS), F32), in...  63.9 us
    unnamed x11, local copies, waits for them, and re-layouts  5.05 us

profile of v1, /device:TPU:1, one launch (start us, length us, event | category | flops | bytes accessed | tf_op | source)
XLA Modules:
  0.0 69.0 jit_solution(17261143132332423366)
XLA Ops:
  0.0 0.0 copy-start
  0.0 1.0 %copy-done = bf16[16,32,512]{2,1,0:T(8,128)(2,1)S(1)} copy-done((bf16[16,32,512]{2,1,0:T(8,128)(2,1)S(1)}, bf16[16,32,512]{2,1,0:T(8,128)(2,1)}, u32[]{:S(2)}) %copy-start) | copy-done | bytes 524312
  1.0 0.0 copy-start.1
  1.0 0.9 %copy-done.1 = bf16[16,16,512]{2,1,0:T(8,128)(2,1)S(1)} copy-done((bf16[16,16,512]{2,1,0:T(8,128)(2,1)S(1)}, bf16[16,16,512]{2,1,0:T(8,128)(2,1)}, u32[]{:S(2)}) %copy-start.1) | copy-done | bytes 262168
  2.0 0.0 copy-start.2
  2.0 0.9 %copy-done.2 = f32[16,3,512]{2,0,1:T(8,128)S(1)} copy-done((f32[16,3,512]{2,0,1:T(8,128)S(1)}, f32[16,3,512]{2,0,1:T(8,128)}, u32[]{:S(2)}) %copy-start.2) | copy-done | bytes 98328
  2.9 0.0 copy-start.3
  2.9 0.7 %copy-done.3 = s32[16,32]{1,0:T(8,128)S(1)} copy-done((s32[16,32]{1,0:T(8,128)S(1)}, s32[16,32]{1,0:T(8,128)}, u32[]{:S(2)}) %copy-start.3) | copy-done | bytes 2072
  3.6 0.0 copy-start.4
  3.6 0.7 copy-done.4
  4.3 63.9 %hmatrix.1 = f32[16,16,512]{2,1,0:T(8,128)S(1)} custom-call(s32[2,64]{1,0:T(2,128)S(1)} %bitcast.4, s32[16,32]{1,0:T(8,128)S(1)} %copy-done.3, s32[2,64]{1,0:T(2,128)S(1)} %bitcast.5, f32[3,16,512]{2,1,0:T(8,128)S(1)} %bitcast.3, bf16[16,16,512]{2,1,0:T(8,128)(2,1)S(1)} %copy-done.1, bf16[16,32,512]{2,1,0:T(8,128)(2,1)S(1)} %copy-done, ...), custom_call_target="tpu_custom_call" | custom-call | tf_op jit(solution)/shard_map/hmatrix/pallas_call | solution.py:291
  68.2 0.8 %copy.8 = f32[16,16,512]{2,1,0:T(8,128)} copy(f32[16,16,512]{2,1,0:T(8,128)S(1)} %hmatrix.1) | data formatting | bytes 1048576
Async XLA Ops:
  0.0 1.0 %copy-start = (bf16[16,32,512]{2,1,0:T(8,128)(2,1)S(1)}, bf16[16,32,512]{2,1,0:T(8,128)(2,1)}, u32[]{:S(2)}) copy-start(bf16[16,32,512]{2,1,0:T(8,128)(2,1)} %basis.1) | copy-start | bytes 1572868
  1.0 0.9 %copy-start.1 = (bf16[16,16,512]{2,1,0:T(8,128)(2,1)S(1)}, bf16[16,16,512]{2,1,0:T(8,128)(2,1)}, u32[]{:S(2)}) copy-start(bf16[16,16,512]{2,1,0:T(8,128)(2,1)} %rhs.1) | copy-start | bytes 786436
  2.0 0.9 %copy-start.2 = (f32[16,3,512]{2,0,1:T(8,128)S(1)}, f32[16,3,512]{2,0,1:T(8,128)}, u32[]{:S(2)}) copy-start(f32[16,3,512]{2,0,1:T(8,128)} %param.6) | copy-start | bytes 294916
  2.9 0.7 %copy-start.3 = (s32[16,32]{1,0:T(8,128)S(1)}, s32[16,32]{1,0:T(8,128)}, u32[]{:S(2)}) copy-start(s32[16,32]{1,0:T(8,128)} %far.1) | copy-start | bytes 6148
  3.6 0.7 copy-start.4

commit v2 on v1

--- a/solution.py
+++ b/solution.py
@@ -27,12 +27,11 @@
     a = pairs[0, s]
     b = pairs[1, s]
     b = jnp.where(b < 0, 4 * CL + a, b)
-    o = b // CL
-    l = b % CL
-    drow = o // 3 - 1
-    wc = o % 3
-    wr = jnp.clip(1 + drow * CL + l, 0, CL + 1)
-    return a, wc, wr
+    o = lax.shift_right_logical(b, 4)
+    l = lax.bitwise_and(b, CL - 1)
+    down = lax.shift_right_logical(o * 11, 5)
+    wr = jnp.clip(1 - CL + down * CL + l, 0, CL + 1)
+    return a, o - 3 * down, wr
 
 
 def make_tile(s, tile, pairs, tables, wc_ref, row0, col0):
@@ -118,8 +117,8 @@
         pltpu.make_async_copy(coupling, cpl, loc_sem.at[3]),
         pltpu.make_async_copy(coords, wc_ref.at[1, :, pl.ds(8, CL)], loc_sem.at[4]),
     ]
-    for c in loads:
-        c.start()
+    for i in (0, 1, 2, 4):
+        loads[i].start()
 
     barrier = pltpu.get_barrier_semaphore()
     partners = [place(row + dr, col + dc) for dr, dc in NEIGHBOURS if dc]
@@ -127,6 +126,7 @@
     partners += [place(row + k, col) for k in range(1, NR)]
     for target in partners:
         pl.semaphore_signal(barrier, inc=1, device_id=target, device_id_type=MESH)
+
     pl.semaphore_wait(barrier, len(partners))
 
     def remote(src, dst, s, r, target):
@@ -156,6 +156,7 @@
             halo.append(remote(src, dst, hs_sem.at[k, i], hr_sem.at[k, i], target))
     for c in halo:
         c.start()
+    loads[3].start()
 
     loads[1].wait()
     loads[2].wait()
@@ -167,11 +168,11 @@
         mine = jnp.zeros((R, 4 * K), F32)
         for i in range(4):
             mine = mine + jnp.where(lane_of == i, full[i * R : (i + 1) * R, :], 0.0)
-        every[row, cy, core, j] = mine.astype(BF)
+        every[row * (NC // 2) + cy, core * 4 + j] = mine.astype(BF)
 
     first = []
     for k in (1, 2, 3):
-        ref = every.at[row, cy, core]
+        ref = every.at[row * (NC // 2) + cy, pl.ds(core * 4, 4)]
         first.append(remote(ref, ref, g1s.at[k - 1], g1r.at[k - 1], place(row, col + 2 * k)))
     for c in first:
         c.start()
@@ -187,19 +188,9 @@
         for g in range(CL):
             tables[g, i] = jnp.broadcast_to(v[:, g : g + 1], (PS, 128))
 
-    for c in first:
-        c.wait()
-    second = []
-    for k in range(1, NR):
-        ref = every.at[row, :, core]
-        second.append(remote(ref, ref, g2s.at[k - 1], g2r.at[k - 1], place(row + k, col)))
-    for c in second:
-        c.start()
-
     loads[4].wait()
     for c in halo:
         c.wait()
-
     tiles = (tile0, tile1)
     build = functools.partial(
         make_tile, pairs=pairs, tables=tables, wc_ref=wc_ref, row0=row, col0=col
@@ -218,14 +209,22 @@
                     build(jnp.minimum(s + 1, NP - 1), tiles[1 - j])
 
     build(0, tile0)
-    cut = NP // 2 * 3 // 4
-    sweep(0, cut)
+    sweep(0, 3)
+    for c in first:
+        c.wait()
+    second = []
+    for k in range(1, NR):
+        ref = every.at[pl.ds(row * (NC // 2), NC // 2), pl.ds(core * 4, 4)]
+        second.append(remote(ref, ref, g2s.at[k - 1], g2r.at[k - 1], place(row + k, col)))
+    for c in second:
+        c.start()
+    sweep(3, 28)
     for c in second:
         c.wait()
-    ref = every.at[:, :, core]
+    ref = every.at[:, pl.ds(core * 4, 4)]
     third = remote(ref, ref, g3s.at[0], g3r.at[0], (row, col + 1 - 2 * core))
     third.start()
-    sweep(cut, NP // 2)
+    sweep(28, NP // 2)
 
     fwd, bwd = slot_codes(pairs_v)
     terms = b_ref[...]
@@ -260,16 +259,16 @@
     third.wait()
     loads[3].wait()
 
-    @pl.loop(0, CL)
+    @pl.loop(0, CL, unroll=2)
     def _(g):
         blocks = []
         for f in range(0, FAR, 4):
             mine = jnp.zeros((R, 4 * K), F32)
             for j in range(4):
                 h = far[g, f + j]
-                d = h // CL
-                got = every[d // NC, (d % NC) // 2, d % 2, (h % CL) // 4].astype(F32)
-                got = pltpu.roll(got, ((j - h % 4 + 4) % 4) * K, 1)
+                at = lax.bitwise_and(lax.shift_right_logical(h, 2), 7)
+                got = every[lax.shift_right_logical(h, 5), at].astype(F32)
+                got = pltpu.roll(got, lax.bitwise_and(j - h, 3) * K, 1)
                 mine = jnp.where(lane_of == j, got, mine)
             blocks.append(mine.astype(BF))
         z = jnp.dot(jnp.concatenate(blocks, axis=1), cpl[g], preferred_element_type=F32)
@@ -285,7 +284,7 @@
 def per_device(coords, rhs, near_pairs, far_list, basis, coupling):
     smem = pl.BlockSpec(memory_space=pltpu.SMEM)
     vmem = pl.BlockSpec(memory_space=pltpu.VMEM)
-    hbm = pl.BlockSpec(memory_space=pl.ANY)
+    hbm = pl.BlockSpec(memory_space=pltpu.HBM)
     dma = pltpu.SemaphoreType.DMA
     pairs = near_pairs.T
     return pl.pallas_call(
@@ -300,7 +299,7 @@
             pltpu.VMEM((CL, K, PS), BF),
             pltpu.VMEM((CL, FAR * K, K), BF),
             pltpu.VMEM((CL, 4, PS, 128), F32),
-            pltpu.VMEM((NR, NC // 2, 2, CL // 4, R, 4 * K), BF),
+            pltpu.VMEM((NR * NC // 2, 2 * CL // 4, R, 4 * K), BF),
             pltpu.VMEM((PS, PS), BF),
             pltpu.VMEM((PS, PS), BF),
             pltpu.VMEM((NP * R, PS), BF),
@@ -321,7 +320,7 @@
             dma((8,)),
         ],
         compiler_params=pltpu.CompilerParams(
-            collective_id=0, has_side_effects=True, vmem_limit_bytes=52 * 2**20
+            collective_id=0, has_side_effects=True, vmem_limit_bytes=63 * 2**20
         ),
         name="hmatrix",
     )(

time: 69.2 us -> 50.8 us (0.73)
  Pallas kernels: 63.9 us -> 48.7 us
  local copies, waits for them, and re-layouts: 5.05 us -> 1.88 us
    pallas_call x1, Pallas kernels: 63.9 us -> 48.7 us  [per_device(): pl.pallas_call(body, out_shape=jax.ShapeDtypeStruct((CL, R, PS), F32), in...]
    unnamed x11 -> x1, local copies, waits for them, and re-layouts: 5.05 us -> 1.88 us
where the time goes in v2:
time: 50.8 us; the launch traced here: 50.6 us
  Pallas kernels  48.7 us (96%)
  local copies, waits for them, and re-layouts  1.88 us (4%)
    pallas_call x1, Pallas kernels, per_device(): pl.pallas_call(body, out_shape=jax.ShapeDtypeStruct((CL, R, PS), F32), in...  48.7 us
    unnamed x1, local copies, waits for them, and re-layouts  1.88 us

profile of v2, /device:TPU:1, one launch (start us, length us, event | category | flops | bytes accessed | tf_op | source)
XLA Modules:
  0.0 50.6 jit_solution(3608909516161845489)
XLA Ops:
  0.0 48.7 %hmatrix.1 = f32[16,16,512]{2,1,0:T(8,128)} custom-call(s32[2,64]{1,0:T(2,128)} %bitcast.5, s32[16,32]{1,0:T(8,128)} %far.1, s32[2,64]{1,0:T(2,128)} %bitcast.6, f32[3,16,512]{2,1,0:T(8,128)} %bitcast.4, bf16[16,16,512]{2,1,0:T(8,128)(2,1)} %rhs.1, bf16[16,32,512]{2,1,0:T(8,128)(2,1)} %basis.1, bf16[16,1024,32]{2,1,0:T(8,128)(2,1)} %bitcast.3), custom_call_target="tpu_custom_call" | custom-call | tf_op jit(solution)/shard_map/hmatrix/pallas_call | solution.py:290
  48.7 1.9 %copy.8 = f32[16,16,512]{2,1,0:T(8,128)} copy(f32[16,16,512]{2,1,0:T(8,128)} %hmatrix.1) | data formatting | bytes 1048576

commit v3 on v2

--- a/solution.py
+++ b/solution.py
@@ -100,8 +100,8 @@
 
 
 def body(
-    pairs, far, pairs_v, coords, rhs, basis, coupling, out,
-    own_c, wc_ref, wr_ref, bas, cpl, tables, every, tile0, tile1, f_ref, b_ref,
+    pairs_h, far_h, coords, rhs, basis, coupling, out,
+    pairs, far, pairs_v, own_c, wc_ref, wr_ref, bas, cpl, tables, every, tile0, tile1, f_ref, b_ref,
     send, back_c, back_r,
     loc_sem, hs_sem, hr_sem, g1s, g1r, g2s, g2r, g3s, g3r, bs_sem, br_sem,
 ):
@@ -116,9 +116,10 @@
         pltpu.make_async_copy(basis, bas, loc_sem.at[2]),
         pltpu.make_async_copy(coupling, cpl, loc_sem.at[3]),
         pltpu.make_async_copy(coords, wc_ref.at[1, :, pl.ds(8, CL)], loc_sem.at[4]),
+        pltpu.make_async_copy(pairs_h, pairs, loc_sem.at[5]),
+        pltpu.make_async_copy(far_h, far, loc_sem.at[6]),
+        pltpu.make_async_copy(pairs_h, pairs_v, loc_sem.at[7]),
     ]
-    for i in (0, 1, 2, 4):
-        loads[i].start()
 
     barrier = pltpu.get_barrier_semaphore()
     partners = [place(row + dr, col + dc) for dr, dc in NEIGHBOURS if dc]
@@ -126,6 +127,8 @@
     partners += [place(row + k, col) for k in range(1, NR)]
     for target in partners:
         pl.semaphore_signal(barrier, inc=1, device_id=target, device_id_type=MESH)
+    for i in (0, 1, 2, 4, 5, 6, 7):
+        loads[i].start()
 
     pl.semaphore_wait(barrier, len(partners))
 
@@ -145,12 +148,12 @@
         elif dr == 1:
             pieces = [
                 (rhs.at[pl.ds(CL - 1, 1)], wr_ref.at[1 - dc, pl.ds(0, 1)]),
-                (coords.at[:, pl.ds(CL - 8, 8)], wc_ref.at[1 - dc, :, pl.ds(0, 8)]),
+                (coords.at[:, pl.ds(CL - 1, 1)], wc_ref.at[1 - dc, :, pl.ds(7, 1)]),
             ]
         else:
             pieces = [
                 (rhs.at[pl.ds(0, 1)], wr_ref.at[1 - dc, pl.ds(CL + 1, 1)]),
-                (coords.at[:, pl.ds(0, 8)], wc_ref.at[1 - dc, :, pl.ds(CL + 8, 8)]),
+                (coords.at[:, pl.ds(0, 1)], wc_ref.at[1 - dc, :, pl.ds(CL + 8, 1)]),
             ]
         for i, (src, dst) in enumerate(pieces):
             halo.append(remote(src, dst, hs_sem.at[k, i], hr_sem.at[k, i], target))
@@ -189,6 +192,7 @@
             tables[g, i] = jnp.broadcast_to(v[:, g : g + 1], (PS, 128))
 
     loads[4].wait()
+    loads[5].wait()
     for c in halo:
         c.wait()
     tiles = (tile0, tile1)
@@ -206,7 +210,7 @@
                 def _():
                     s = 2 * i + j
                     use(s, tiles[j])
-                    build(jnp.minimum(s + 1, NP - 1), tiles[1 - j])
+                    build(s + 1, tiles[1 - j])
 
     build(0, tile0)
     sweep(0, 3)
@@ -224,42 +228,47 @@
     ref = every.at[:, pl.ds(core * 4, 4)]
     third = remote(ref, ref, g3s.at[0], g3r.at[0], (row, col + 1 - 2 * core))
     third.start()
-    sweep(28, NP // 2)
-
-    fwd, bwd = slot_codes(pairs_v)
+    sweep(28, NP // 2 - 1)
+    use(NP - 2, tile0)
+    build(NP - 1, tile1)
+    use(NP - 1, tile1)
+
+    loads[7].wait()
+    fwd, bwd = slot_codes(pairs_v[...])
     terms = b_ref[...]
     back = []
 
-    def give(k):
-        dr, dc = NEIGHBOURS[k]
-        target = place(row + dr, col + dc)
+    def give(k, dr, dc):
         if dr == 0:
             src, dst = send.at[dc + 1, pl.ds(1, CL)], back_c.at[k]
         else:
             src = send.at[dc + 1, pl.ds(0 if dr < 0 else CL + 1, 1)]
             dst = back_r.at[pl.ds(k - 2, 1)]
-        c = remote(src, dst, bs_sem.at[k], br_sem.at[k], target)
+        c = remote(src, dst, bs_sem.at[k], br_sem.at[k], place(row + dr, col + dc))
         c.start()
         back.append(c)
 
     wide = (CL + 2) * R
-    for dc, ks in ((-1, (0, 2, 5)), (1, (1, 4, 7))):
+    for side in (core, 1 - core):
+        dc = 2 * side - 1
         part = jnp.dot(one_hot(bwd, (dc + 1) * wide, wide), terms, preferred_element_type=F32)
         send[dc + 1] = part.astype(BF).reshape(CL + 2, R, PS)
-        for k in ks:
-            give(k)
-    for at, k in ((0, 3), (CL + 1, 6)):
+        give(side, 0, dc)
+        give(2 + 2 * side, -1, dc)
+        give(5 + 2 * side, 1, dc)
+    for at, k, dr in ((0, 3, -1), (CL + 1, 6, 1)):
         part = jnp.dot(one_hot(bwd, wide + at * R, R), terms, preferred_element_type=F32)
         send[1, at] = part.astype(BF)
-        give(k)
+        give(k, dr, 0)
     near = jnp.dot(one_hot(bwd, wide + R, CL * R), terms, preferred_element_type=F32)
     near = near + jnp.dot(one_hot(fwd, 0, CL * R), f_ref[...], preferred_element_type=F32)
     out[...] = near.reshape(CL, R, PS)
 
     third.wait()
     loads[3].wait()
-
-    @pl.loop(0, CL, unroll=2)
+    loads[6].wait()
+
+    @pl.loop(0, CL, unroll=4)
     def _(g):
         blocks = []
         for f in range(0, FAR, 4):
@@ -282,17 +291,21 @@
 
 
 def per_device(coords, rhs, near_pairs, far_list, basis, coupling):
-    smem = pl.BlockSpec(memory_space=pltpu.SMEM)
     vmem = pl.BlockSpec(memory_space=pltpu.VMEM)
     hbm = pl.BlockSpec(memory_space=pltpu.HBM)
     dma = pltpu.SemaphoreType.DMA
-    pairs = near_pairs.T
+    def hold(x):
+        return pltpu.with_memory_space_constraint(x, pltpu.HBM)
+
     return pl.pallas_call(
         body,
-        out_shape=jax.ShapeDtypeStruct((CL, R, PS), F32),
-        in_specs=[smem, smem, vmem, hbm, hbm, hbm, hbm],
+        out_shape=pltpu.VMEM((CL, R, PS), F32),
+        in_specs=[hbm] * 6,
         out_specs=vmem,
         scratch_shapes=[
+            pltpu.SMEM((2, NP), jnp.int32),
+            pltpu.SMEM((CL, FAR), jnp.int32),
+            pltpu.VMEM((2, NP), jnp.int32),
             pltpu.VMEM((3, CL, PS), F32),
             pltpu.VMEM((3, 3, CL + 16, PS), F32),
             pltpu.VMEM((3, CL + 2, R, PS), BF),
@@ -307,7 +320,7 @@
             pltpu.VMEM((3, CL + 2, R, PS), BF),
             pltpu.VMEM((2, CL, R, PS), BF),
             pltpu.VMEM((6, R, PS), BF),
-            dma((5,)),
+            dma((8,)),
             dma((8, 2)),
             dma((8, 2)),
             dma((3,)),
@@ -320,17 +333,16 @@
             dma((8,)),
         ],
         compiler_params=pltpu.CompilerParams(
-            collective_id=0, has_side_effects=True, vmem_limit_bytes=63 * 2**20
+            collective_id=0, has_side_effects=True, vmem_limit_bytes=62 * 2**20
         ),
         name="hmatrix",
     )(
-        pairs,
-        far_list,
-        pairs,
-        coords.transpose(1, 0, 2),
-        rhs,
-        basis,
-        coupling.reshape(CL, FAR * K, K),
+        hold(near_pairs.T),
+        hold(far_list),
+        hold(coords.transpose(1, 0, 2)),
+        hold(rhs),
+        hold(basis),
+        hold(coupling.reshape(CL, FAR * K, K)),
     )
 
 

time: 50.8 us -> 46.4 us (0.913)
  Pallas kernels: 48.7 us -> 44.9 us
  local copies, waits for them, and re-layouts: 1.88 us -> 0.8 us
    pallas_call x1, Pallas kernels: 48.7 us -> 44.9 us  [per_device(): pl.pallas_call(body, out_shape=pltpu.VMEM((CL, R, PS), F32), in_specs=[hb...]
    unnamed x1, local copies, waits for them, and re-layouts: 1.88 us -> 0.8 us
where the time goes in v3:
time: 46.4 us; the launch traced here: 45.8 us
  Pallas kernels  44.9 us (97%)
  local copies, waits for them, and re-layouts  0.8 us (2%)
    pallas_call x1, Pallas kernels, per_device(): pl.pallas_call(body, out_shape=pltpu.VMEM((CL, R, PS), F32), in_specs=[hb...  44.9 us

profile of v3, /device:TPU:1, one launch (start us, length us, event | category | flops | bytes accessed | tf_op | source)
XLA Modules:
  0.0 45.8 jit_solution(9072608492361730225)
XLA Ops:
  0.0 44.9 %hmatrix.1 = f32[16,16,512]{2,1,0:T(8,128)S(1)} custom-call(s32[2,64]{1,0:T(2,128)} %bitcast.5, s32[16,32]{1,0:T(8,128)} %far_h.1, f32[3,16,512]{2,1,0:T(8,128)} %bitcast.4, bf16[16,16,512]{2,1,0:T(8,128)(2,1)} %rhs.1, bf16[16,32,512]{2,1,0:T(8,128)(2,1)} %basis.1, bf16[16,1024,32]{2,1,0:T(8,128)(2,1)} %bitcast.3), custom_call_target="tpu_custom_call" | custom-call | tf_op jit(solution)/shard_map/hmatrix/pallas_call | solution.py:300
  45.0 0.8 %copy.8 = f32[16,16,512]{2,1,0:T(8,128)} copy(f32[16,16,512]{2,1,0:T(8,128)S(1)} %hmatrix.1) | data formatting | bytes 1048576

commit v4 on v3

--- a/solution.py
+++ b/solution.py
@@ -19,8 +19,9 @@
 NEIGHBOURS = [(0, -1), (0, 1), (-1, -1), (-1, 0), (-1, 1), (1, -1), (1, 0), (1, 1)]
 
 
-def place(row, col):
-    return (lax.rem(row + NR, NR), lax.rem(col + NC, NC))
+def inside(row, col):
+    rows = jnp.logical_and(row >= 0, row < NR)
+    return jnp.logical_and(rows, jnp.logical_and(col >= 0, col < NC))
 
 
 def pair_ids(pairs, s):
@@ -101,7 +102,7 @@
 
 def body(
     pairs_h, far_h, coords, rhs, basis, coupling, out,
-    pairs, far, pairs_v, own_c, wc_ref, wr_ref, bas, cpl, tables, every, tile0, tile1, f_ref, b_ref,
+    pairs, far, pairs_v, own_c, wc_ref, wr_ref, bas, cpl, tables, every, tile0, tile1, f_ref, b_ref, hot_f, hot_b, picked,
     send, back_c, back_r,
     loc_sem, hs_sem, hr_sem, g1s, g1r, g2s, g2r, g3s, g3r, bs_sem, br_sem,
 ):
@@ -122,43 +123,53 @@
     ]
 
     barrier = pltpu.get_barrier_semaphore()
-    partners = [place(row + dr, col + dc) for dr, dc in NEIGHBOURS if dc]
-    partners += [place(row, col + 2 * k) for k in (1, 2, 3)]
-    partners += [place(row + k, col) for k in range(1, NR)]
-    for target in partners:
+    x, z = lax.rem(row, 4), row // 4
+    y_peers = [(row, lax.rem(col + 2 * k, NC)) for k in (1, 2, 3)]
+    x_peers = [(z * 4 + lax.rem(x + k, 4), col) for k in (1, 2, 3)]
+    z_peers = [(lax.rem(z + k, 4) * 4 + x, col) for k in (1, 2, 3)]
+    count = jnp.int32(9)
+    for dr, dc in NEIGHBOURS:
+        there = inside(row + dr, col + dc)
+        count = count + there.astype(jnp.int32)
+
+        @pl.when(there)
+        def _():
+            pl.semaphore_signal(
+                barrier, inc=1, device_id=(row + dr, col + dc), device_id_type=MESH
+            )
+
+    for target in y_peers + x_peers + z_peers:
         pl.semaphore_signal(barrier, inc=1, device_id=target, device_id_type=MESH)
     for i in (0, 1, 2, 4, 5, 6, 7):
         loads[i].start()
 
-    pl.semaphore_wait(barrier, len(partners))
+    pl.semaphore_wait(barrier, count)
 
     def remote(src, dst, s, r, target):
         return pltpu.make_async_remote_copy(
             src_ref=src, dst_ref=dst, send_sem=s, recv_sem=r, device_id=target, device_id_type=MESH
         )
 
-    halo = []
-    for k, (dr, dc) in enumerate(NEIGHBOURS):
-        target = place(row + dr, col + dc)
+    def lend(k, dr, dc, i):
         if dr == 0:
-            pieces = [
-                (rhs, wr_ref.at[1 - dc, pl.ds(1, CL)]),
-                (coords, wc_ref.at[1 - dc, :, pl.ds(8, CL)]),
-            ]
-        elif dr == 1:
-            pieces = [
-                (rhs.at[pl.ds(CL - 1, 1)], wr_ref.at[1 - dc, pl.ds(0, 1)]),
-                (coords.at[:, pl.ds(CL - 1, 1)], wc_ref.at[1 - dc, :, pl.ds(7, 1)]),
-            ]
+            own, near = pl.ds(0, CL), pl.ds(1, CL)
+        elif dr > 0:
+            own, near = pl.ds(CL - 1, 1), pl.ds(0, 1)
         else:
-            pieces = [
-                (rhs.at[pl.ds(0, 1)], wr_ref.at[1 - dc, pl.ds(CL + 1, 1)]),
-                (coords.at[:, pl.ds(0, 1)], wc_ref.at[1 - dc, :, pl.ds(CL + 8, 1)]),
-            ]
-        for i, (src, dst) in enumerate(pieces):
-            halo.append(remote(src, dst, hs_sem.at[k, i], hr_sem.at[k, i], target))
-    for c in halo:
-        c.start()
+            own, near = pl.ds(0, 1), pl.ds(CL + 1, 1)
+        if i == 0:
+            at = pl.ds(near.start + 7, near.size)
+            src, dst = coords.at[:, own], wc_ref.at[1 - dc, :, at]
+        else:
+            src, dst = rhs.at[own], wr_ref.at[1 - dc, near]
+        return remote(src, dst, hs_sem.at[k, i], hr_sem.at[k, i], (row + dr, col + dc))
+
+    slow, fast = 2 * core - 1, 1 - 2 * core
+    for i in range(2):
+        pl.when(inside(row, col + slow))(lend(core, 0, slow, i).start)
+        for k, (dr, dc) in list(enumerate(NEIGHBOURS))[2:]:
+            pl.when(inside(row + dr, col + dc))(lend(k, dr, dc, i).start)
+        pl.when(inside(row, col + fast))(lend(1 - core, 0, fast, i).start)
     loads[3].start()
 
     loads[1].wait()
@@ -176,7 +187,7 @@
     first = []
     for k in (1, 2, 3):
         ref = every.at[row * (NC // 2) + cy, pl.ds(core * 4, 4)]
-        first.append(remote(ref, ref, g1s.at[k - 1], g1r.at[k - 1], place(row, col + 2 * k)))
+        first.append(remote(ref, ref, g1s.at[k - 1], g1r.at[k - 1], y_peers[k - 1]))
     for c in first:
         c.start()
 
@@ -191,10 +202,15 @@
         for g in range(CL):
             tables[g, i] = jnp.broadcast_to(v[:, g : g + 1], (PS, 128))
 
+    loads[7].wait()
+    fwd, bwd = slot_codes(pairs_v[...])
+    hot_f[...] = one_hot(fwd, 0, CL * R)
+    wide = (CL + 2) * R
+    for i in range(3):
+        hot_b[i * wide : (i + 1) * wide, :] = one_hot(bwd, i * wide, wide)
+
     loads[4].wait()
     loads[5].wait()
-    for c in halo:
-        c.wait()
     tiles = (tile0, tile1)
     build = functools.partial(
         make_tile, pairs=pairs, tables=tables, wc_ref=wc_ref, row0=row, col0=col
@@ -212,17 +228,41 @@
                     use(s, tiles[j])
                     build(s + 1, tiles[1 - j])
 
+    def settle(copies):
+        for (dr, dc), c in zip(NEIGHBOURS, copies):
+            pl.when(inside(row + dr, col + dc))(c.wait_send)
+            pl.when(inside(row - dr, col - dc))(c.wait_recv)
+
+    settle([lend(k, dr, dc, 0) for k, (dr, dc) in enumerate(NEIGHBOURS)])
     build(0, tile0)
-    sweep(0, 3)
+    settle([lend(k, dr, dc, 1) for k, (dr, dc) in enumerate(NEIGHBOURS)])
+    sweep(0, 2)
     for c in first:
         c.wait()
+    def blend(zero, one):
+        return zero * (1 - core) + one * core
+
     second = []
-    for k in range(1, NR):
-        ref = every.at[pl.ds(row * (NC // 2), NC // 2), pl.ds(core * 4, 4)]
-        second.append(remote(ref, ref, g2s.at[k - 1], g2r.at[k - 1], place(row + k, col)))
+    ref = every.at[pl.ds(row * 4, 4), pl.ds(core * 4, 4)]
+    for k in range(3):
+        target = (blend(x_peers[k][0], z_peers[k][0]), col)
+        second.append(remote(ref, ref, g2s.at[k], g2r.at[k], target))
     for c in second:
         c.start()
-    sweep(3, 28)
+    sweep(2, 6)
+    for c in second:
+        c.wait()
+    second = []
+    for m in range(4):
+        at = blend(z * 16 + m * 4, m * 16 + x * 4)
+        ref = every.at[pl.ds(at, 4), pl.ds(core * 4, 4)]
+        for k in range(3):
+            target = (blend(z_peers[k][0], x_peers[k][0]), col)
+            n = 3 + 3 * m + k
+            second.append(remote(ref, ref, g2s.at[n], g2r.at[n], target))
+    for c in second:
+        c.start()
+    sweep(6, 28)
     for c in second:
         c.wait()
     ref = every.at[:, pl.ds(core * 4, 4)]
@@ -233,35 +273,32 @@
     build(NP - 1, tile1)
     use(NP - 1, tile1)
 
-    loads[7].wait()
-    fwd, bwd = slot_codes(pairs_v[...])
     terms = b_ref[...]
-    back = []
-
-    def give(k, dr, dc):
+
+    def owed(k, dr, dc):
         if dr == 0:
             src, dst = send.at[dc + 1, pl.ds(1, CL)], back_c.at[k]
         else:
             src = send.at[dc + 1, pl.ds(0 if dr < 0 else CL + 1, 1)]
             dst = back_r.at[pl.ds(k - 2, 1)]
-        c = remote(src, dst, bs_sem.at[k], br_sem.at[k], place(row + dr, col + dc))
-        c.start()
-        back.append(c)
-
-    wide = (CL + 2) * R
+        return remote(src, dst, bs_sem.at[k], br_sem.at[k], (row + dr, col + dc))
+
+    def give(k, dr, dc):
+        pl.when(inside(row + dr, col + dc))(owed(k, dr, dc).start)
+
     for side in (core, 1 - core):
         dc = 2 * side - 1
-        part = jnp.dot(one_hot(bwd, (dc + 1) * wide, wide), terms, preferred_element_type=F32)
+        part = jnp.dot(hot_b[pl.ds(pl.multiple_of((dc + 1) * wide, R), wide), :], terms, preferred_element_type=F32)
         send[dc + 1] = part.astype(BF).reshape(CL + 2, R, PS)
         give(side, 0, dc)
         give(2 + 2 * side, -1, dc)
         give(5 + 2 * side, 1, dc)
     for at, k, dr in ((0, 3, -1), (CL + 1, 6, 1)):
-        part = jnp.dot(one_hot(bwd, wide + at * R, R), terms, preferred_element_type=F32)
+        part = jnp.dot(hot_b[wide + at * R : wide + (at + 1) * R, :], terms, preferred_element_type=F32)
         send[1, at] = part.astype(BF)
         give(k, dr, 0)
-    near = jnp.dot(one_hot(bwd, wide + R, CL * R), terms, preferred_element_type=F32)
-    near = near + jnp.dot(one_hot(fwd, 0, CL * R), f_ref[...], preferred_element_type=F32)
+    near = jnp.dot(hot_b[wide + R : wide + R + CL * R, :], terms, preferred_element_type=F32)
+    near = near + jnp.dot(hot_f[...], f_ref[...], preferred_element_type=F32)
     out[...] = near.reshape(CL, R, PS)
 
     third.wait()
@@ -270,7 +307,6 @@
 
     @pl.loop(0, CL, unroll=4)
     def _(g):
-        blocks = []
         for f in range(0, FAR, 4):
             mine = jnp.zeros((R, 4 * K), F32)
             for j in range(4):
@@ -279,15 +315,22 @@
                 got = every[lax.shift_right_logical(h, 5), at].astype(F32)
                 got = pltpu.roll(got, lax.bitwise_and(j - h, 3) * K, 1)
                 mine = jnp.where(lane_of == j, got, mine)
-            blocks.append(mine.astype(BF))
-        z = jnp.dot(jnp.concatenate(blocks, axis=1), cpl[g], preferred_element_type=F32)
-        out[g] += jnp.dot(z.astype(BF), bas[g], preferred_element_type=F32)
-
-    for c in back:
-        c.wait()
-    out[...] += back_c[0].astype(F32) + back_c[1].astype(F32)
-    out[CL - 1] += back_r[0].astype(F32) + back_r[1].astype(F32) + back_r[2].astype(F32)
-    out[0] += back_r[3].astype(F32) + back_r[4].astype(F32) + back_r[5].astype(F32)
+            picked[g, :, f * K : (f + 4) * K] = mine.astype(BF)
+
+    inner = [jnp.dot(picked[g], cpl[g], preferred_element_type=F32).astype(BF) for g in range(CL)]
+    for g in range(CL):
+        out[g] += jnp.dot(inner[g], bas[g], preferred_element_type=F32)
+
+    settle([owed(k, dr, dc) for k, (dr, dc) in enumerate(NEIGHBOURS)])
+    for k, (dr, dc) in enumerate(NEIGHBOURS):
+
+        @pl.when(inside(row - dr, col - dc))
+        def _():
+            if dr == 0:
+                out[...] += back_c[k].astype(F32)
+            else:
+                at = CL - 1 if dr < 0 else 0
+                out[at] += back_r[k - 2].astype(F32)
 
 
 def per_device(coords, rhs, near_pairs, far_list, basis, coupling):
@@ -317,6 +360,9 @@
             pltpu.VMEM((PS, PS), BF),
             pltpu.VMEM((NP * R, PS), BF),
             pltpu.VMEM((NP * R, PS), BF),
+            pltpu.VMEM((CL * R, NP * R), BF),
+            pltpu.VMEM((3 * (CL + 2) * R, NP * R), BF),
+            pltpu.VMEM((CL, R, FAR * K), BF),
             pltpu.VMEM((3, CL + 2, R, PS), BF),
             pltpu.VMEM((2, CL, R, PS), BF),
             pltpu.VMEM((6, R, PS), BF),
@@ -325,8 +371,8 @@
             dma((8, 2)),
             dma((3,)),
             dma((3,)),
-            dma((NR - 1,)),
-            dma((NR - 1,)),
+            dma((15,)),
+            dma((15,)),
             dma((1,)),
             dma((1,)),
             dma((8,)),

time: 46.4 us -> 45.9 us (0.989); the launches traced: 45.8 us -> 45.8 us
  no operation moved by 1% of the time
where the time goes in v4:
time: 45.9 us; the launch traced here: 45.8 us
  Pallas kernels  45 us (98%)
  local copies, waits for them, and re-layouts  0.8 us (2%)
    pallas_call x1, Pallas kernels, per_device(): pl.pallas_call(body, out_shape=pltpu.VMEM((CL, R, PS), F32), in_specs=[hb...  45 us

profile of v4, /device:TPU:1, one launch (start us, length us, event | category | flops | bytes accessed | tf_op | source)
XLA Modules:
  0.0 45.8 jit_solution(6569470709110304841)
XLA Ops:
  0.0 45.0 %hmatrix.1 = f32[16,16,512]{2,1,0:T(8,128)S(1)} custom-call(s32[2,64]{1,0:T(2,128)} %bitcast.5, s32[16,32]{1,0:T(8,128)} %far_h.1, f32[3,16,512]{2,1,0:T(8,128)} %bitcast.4, bf16[16,16,512]{2,1,0:T(8,128)(2,1)} %rhs.1, bf16[16,32,512]{2,1,0:T(8,128)(2,1)} %basis.1, bf16[16,1024,32]{2,1,0:T(8,128)(2,1)} %bitcast.3), custom_call_target="tpu_custom_call" | custom-call | tf_op jit(solution)/shard_map/hmatrix/pallas_call | solution.py:343
  45.0 0.8 %copy.8 = f32[16,16,512]{2,1,0:T(8,128)} copy(f32[16,16,512]{2,1,0:T(8,128)S(1)} %hmatrix.1) | data formatting | bytes 1048576

commit v5 on v4

--- a/solution.py
+++ b/solution.py
@@ -236,7 +236,7 @@
     settle([lend(k, dr, dc, 0) for k, (dr, dc) in enumerate(NEIGHBOURS)])
     build(0, tile0)
     settle([lend(k, dr, dc, 1) for k, (dr, dc) in enumerate(NEIGHBOURS)])
-    sweep(0, 2)
+    sweep(0, 4)
     for c in first:
         c.wait()
     def blend(zero, one):
@@ -249,7 +249,7 @@
         second.append(remote(ref, ref, g2s.at[k], g2r.at[k], target))
     for c in second:
         c.start()
-    sweep(2, 6)
+    sweep(4, 10)
     for c in second:
         c.wait()
     second = []
@@ -262,13 +262,13 @@
             second.append(remote(ref, ref, g2s.at[n], g2r.at[n], target))
     for c in second:
         c.start()
-    sweep(6, 28)
+    sweep(10, 30)
     for c in second:
         c.wait()
     ref = every.at[:, pl.ds(core * 4, 4)]
     third = remote(ref, ref, g3s.at[0], g3r.at[0], (row, col + 1 - 2 * core))
     third.start()
-    sweep(28, NP // 2 - 1)
+    sweep(30, NP // 2 - 1)
     use(NP - 2, tile0)
     build(NP - 1, tile1)
     use(NP - 1, tile1)

time: 45.9 us -> 44 us (0.959)
  Pallas kernels: 45 us -> 43.1 us
    pallas_call x1, Pallas kernels: 45 us -> 43.1 us  [per_device(): pl.pallas_call(body, out_shape=pltpu.VMEM((CL, R, PS), F32), in_specs=[hb...]
where the time goes in v5:
time: 44 us; the launch traced here: 43.9 us
  Pallas kernels  43.1 us (98%)
  local copies, waits for them, and re-layouts  0.8 us (2%)
    pallas_call x1, Pallas kernels, per_device(): pl.pallas_call(body, out_shape=pltpu.VMEM((CL, R, PS), F32), in_specs=[hb...  43.1 us

profile of v5, /device:TPU:1, one launch (start us, length us, event | category | flops | bytes accessed | tf_op | source)
XLA Modules:
  0.0 43.9 jit_solution(3081278476089245370)
XLA Ops:
  0.0 43.1 %hmatrix.1 = f32[16,16,512]{2,1,0:T(8,128)S(1)} custom-call(s32[2,64]{1,0:T(2,128)} %bitcast.5, s32[16,32]{1,0:T(8,128)} %far_h.1, f32[3,16,512]{2,1,0:T(8,128)} %bitcast.4, bf16[16,16,512]{2,1,0:T(8,128)(2,1)} %rhs.1, bf16[16,32,512]{2,1,0:T(8,128)(2,1)} %basis.1, bf16[16,1024,32]{2,1,0:T(8,128)(2,1)} %bitcast.3), custom_call_target="tpu_custom_call" | custom-call | tf_op jit(solution)/shard_map/hmatrix/pallas_call | solution.py:343
  43.1 0.8 %copy.8 = f32[16,16,512]{2,1,0:T(8,128)} copy(f32[16,16,512]{2,1,0:T(8,128)S(1)} %hmatrix.1) | data formatting | bytes 1048576
